TPU v7x, 32 devices: a whole 2x2x4 slice. The times are simulated.
32 devices in a mesh: station: 8 (over y, x, core), section: 4 (over z).
Axes of the slice: x: 2, y: 2, z: 4, core: 2. Of those that a mesh axis runs over, the one named last changes fastest.
Arguments:
- voltages: bfloat16 [8, 128, 17408], P('station', 'section'), may hold values from -6 to 6
- taper: float32 [14, 1024], replicated, may hold values from -1.6 to 1.6
- beam_weight_table: bfloat16 [8, 8, 128, 2, 512], P('station', None, 'section'), may hold values from -1 to 1
- starts: int32 [8], replicated, may hold values from 0 to 3
- owner_map: int32 [512], replicated, may hold values from 0 to 7, as said below
Outputs:
- visibilities: bfloat16 [4, 8, 16, 8, 4, 16, 32], P('section', 'station')
Inputs may be any that keep to these rules, and one draw needn't show every extreme that they name: `owner_map`: within each block of 128 consecutive channels every owner 0 to 7 owns exactly 16 channels.
All inputs are finite; a program needn't handle non-finite values.
Results may differ from a plain program's by a relative error of at most 0.014.
Values may be sent and summed in bfloat16 or wider, within the bound.
A program may use at most 64 MiB of HBM per device.

v0:
```python
import math

import jax
import jax.numpy as jnp
from jax import lax
from jax.sharding import PartitionSpec as P


def dft_table(length):
    half = length // 2
    index_n = jnp.arange(length, dtype=jnp.int32)[:, None]
    index_k = jnp.arange(half, dtype=jnp.int32)[None, :]
    phase = (index_n * index_k % length).astype(jnp.float32) * (2.0 * math.pi / length)
    factor = 1.0 / math.sqrt(length)
    return jnp.concatenate([jnp.cos(phase) * factor, -jnp.sin(phase) * factor], axis=1).astype(
        jnp.bfloat16
    )


def local(voltages, taper, beam_weight_table, starts, owner_map):
    inputs = voltages.shape[1]
    length = taper.shape[1]
    tap_count = taper.shape[0]
    frames = voltages.shape[2] // length - tap_count + 1
    channels = length // 2
    beam_count = beam_weight_table.shape[1]
    antennas = inputs // 2
    sections = lax.axis_size("section")
    stations = lax.axis_size("station")
    section = lax.axis_index("section")
    span_count = max(1, sections // 2)
    block = channels // sections
    per_owner = block // stations
    framed = voltages[0].reshape(inputs, frames + tap_count - 1, length)
    filtered = jnp.zeros((inputs, frames, length), jnp.float32)
    for tap in range(tap_count):
        filtered = filtered + taper[tap][None, None, :] * framed[:, tap : tap + frames, :].astype(
            jnp.float32
        )
    rows = filtered.astype(jnp.bfloat16).reshape(inputs * frames, length)
    spectra = jnp.dot(rows, dft_table(length), preferred_element_type=jnp.float32)
    spectra = spectra.reshape(antennas, 2, frames, 2, channels)
    real_x = spectra[:, :, :, 0, :]
    imag_x = spectra[:, :, :, 1, :]
    offset = jnp.remainder(section - starts, sections)
    inside = (offset < span_count).astype(jnp.float32)
    scaled = beam_weight_table[0].astype(jnp.float32).reshape(beam_count, antennas, 2, 2, channels)
    scaled = scaled * inside[:, None, None, None, None]
    real_w = scaled[:, :, :, 0, :]
    imag_w = scaled[:, :, :, 1, :]
    real_b = jnp.einsum("bapk,apfk->kbpf", real_w, real_x) - jnp.einsum(
        "bapk,apfk->kbpf", imag_w, imag_x
    )
    imag_b = jnp.einsum("bapk,apfk->kbpf", real_w, imag_x) + jnp.einsum(
        "bapk,apfk->kbpf", imag_w, real_x
    )
    partial_sum = jnp.stack([real_b, imag_b], axis=3).reshape(channels, beam_count * 4 * frames)
    mine = lax.psum_scatter(partial_sum, "section", scatter_dimension=0, tiled=True).astype(
        jnp.bfloat16
    )
    owners_here = lax.dynamic_slice_in_dim(owner_map, section * block, block, 0)
    ranked = jnp.argsort(owners_here, stable=True)
    placed = jnp.take(mine, ranked, axis=0)
    arrived = lax.all_to_all(placed, "station", split_axis=0, concat_axis=0, tiled=True)
    gathered = arrived.reshape(stations, per_owner, beam_count, 2, 2, frames)
    gathered = jnp.transpose(gathered, (1, 2, 5, 0, 3, 4)).astype(jnp.float32)
    real_z = gathered[..., 0].reshape(per_owner, beam_count, frames, 2 * stations)
    imag_z = gathered[..., 1].reshape(per_owner, beam_count, frames, 2 * stations)
    real_v = jnp.einsum("cbfi,cbfj->cbfij", real_z, real_z) + jnp.einsum(
        "cbfi,cbfj->cbfij", imag_z, imag_z
    )
    imag_v = jnp.einsum("cbfi,cbfj->cbfij", imag_z, real_z) - jnp.einsum(
        "cbfi,cbfj->cbfij", real_z, imag_z
    )
    visible = jnp.concatenate([real_v, imag_v], axis=-1).astype(jnp.bfloat16)
    return visible.reshape(1, 1, per_owner, beam_count, frames, 2 * stations, 4 * stations)


def solution(mesh):
    placed = (
        P("station", "section", None),
        P(),
        P("station", None, "section", None, None),
        P(),
        P(),
    )
    return jax.shard_map(
        local,
        mesh=mesh,
        in_specs=placed,
        out_specs=P("section", "station", None, None, None, None, None),
        check_vma=False,
    )
```

profile of v0, /device:TPU:0, one launch (start us, length us, event | category | flops | bytes accessed | tf_op | source)
XLA Modules:
  0.0 91.2 jit_solution(5529574777310219491)
XLA Ops:
  6.5 9.2 %multiply_convert_fusion = (bf16[1024,512]{0,1:T(8,128)(2,1)S(1)}, bf16[1024,512]{0,1:T(8,128)(2,1)}) fusion(), kind=kLoop, calls=%fused_computation.23 | loop fusion | flops 9961472 | bytes 2097152 | tf_op jit(solution)/shard_map/convert.18
  15.8 1.7 %reshape_squeeze.2 = bf16[32,17,1024]{2,1,0:T(8,128)(2,1)S(1)} reshape(bf16[1,32,17408]{2,1,0:T(8,128)(2,1)} %param.5) | data formatting | bytes 2228224 | tf_op jit(solution)/shard_map/reshape;squeeze | solution.py:34
  17.5 1.4 %pad_maximum_fusion.1 = bf16[1024,1024]{0,1:T(8,128)(2,1)S(1)} fusion(bf16[1024,512]{0,1:T(8,128)(2,1)S(1)} %get-tuple-element.27, bf16[1024,512]{0,1:T(8,128)(2,1)} %get-tuple-element.28), kind=kLoop, calls=%fused_computation.19 | loop fusion | flops 4194304 | bytes 4194304 | tf_op jit(solution)/shard_map/concatenate | solution.py:15
  18.9 2.0 %add_convert_fusion.1 = bf16[32,4,1024]{2,1,0:T(4,128)(2,1)S(1)} fusion(bf16[32,17,1024]{2,1,0:T(8,128)(2,1)S(1)} %reshape_squeeze.2, f32[1024]{0:T(1024)S(1)} %bitcast.86, f32[1024]{0:T(1024)S(1)} %bitcast.87, f32[1024]{0:T(1024)S(1)} %bitcast.75, f32[1024]{0:T(1024)S(1)} %bitcast.76, f32[1024]{0:T(1024)S(1)} %bitcast.77, f32[1024]{0:T(1024)S(1)} %bitcast.78, ...), kind=kLoop, calls=%fused_computation.28 | loop fusion | flops 5505024 | bytes 3989504 | tf_op jit(solution)/shard_map/convert_element_type | solution.py:40
  20.9 0.9 fusion.12
  21.7 0.7 copy.49
  22.9 5.3 %copy.48 = f32[8,16,2,2,512]{1,0,2,4,3:T(8,128)} copy(bf16[8,16,2,2,512]{4,0,3,2,1:T(8,128)(2,1)S(1)} %bitcast.67) | data formatting | bytes 1572864 | tf_op jit(solution)/shard_map/convert_element_type | solution.py:47
  28.2 0.7 copy.50
  28.9 4.1 %broadcast_multiply_fusion = bf16[8,16,2,2,512]{1,0,2,4,3:T(8,128)(2,1)S(1)} fusion(f32[8,16,2,2,512]{1,0,2,4,3:T(8,128)} %copy.48, f32[8]{0:T(128)S(1)} %compare_convert_fusion), kind=kLoop, calls=%fused_computation.6 | loop fusion | flops 524288 | bytes 1572896 | tf_op jit(solution)/shard_map/mul | solution.py:48
  33.0 1.3 %fusion.1 = f32[512,2,4,8]{3,2,1,0:T(4,128)S(1)} fusion(bf16[16,2,4,512]{0,2,1,3:T(4,128)(2,1)S(1)} %copy.49, bf16[8,16,2,2,512]{1,0,2,4,3:T(8,128)(2,1)S(1)} %broadcast_multiply_fusion), kind=kOutput, calls=%fused_computation.8 | convolution fusion | flops 1048576 | bytes 3276800 | tf_op jit(solution)/shard_map/bapk,apfk->kbpf/dot_general | solution.py:51
  34.3 1.3 %fusion = f32[512,2,4,8]{3,2,1,0:T(4,128)S(1)} fusion(bf16[16,2,4,512]{0,2,1,3:T(4,128)(2,1)S(1)} %copy.50, bf16[8,16,2,2,512]{1,0,2,4,3:T(8,128)(2,1)S(1)} %broadcast_multiply_fusion), kind=kOutput, calls=%fused_computation.7 | convolution fusion | flops 1048576 | bytes 3276800 | tf_op jit(solution)/shard_map/bapk,apfk->kbpf/dot_general | solution.py:54
  35.6 1.3 %subtract_bitcast_fusion = f32[512,8,2,1,4]{1,4,2,0,3:T(4,128)S(1)} fusion(f32[512,2,4,8]{3,2,1,0:T(4,128)S(1)} %fusion.1, bf16[16,2,4,512]{0,2,1,3:T(4,128)(2,1)S(1)} %copy.50, bf16[8,16,2,2,512]{1,0,2,4,3:T(8,128)(2,1)S(1)} %broadcast_multiply_fusion), kind=kOutput, calls=%fused_computation.22 | convolution fusion | flops 1081344 | bytes 5373952 | tf_op jit(solution)/shard_map/bapk,apfk->kbpf/dot_general | solution.py:51
  36.9 1.3 %add_bitcast_fusion = f32[512,8,2,1,4]{1,4,2,0,3:T(4,128)S(1)} fusion(f32[512,2,4,8]{3,2,1,0:T(4,128)S(1)} %fusion, bf16[16,2,4,512]{0,2,1,3:T(4,128)(2,1)S(1)} %copy.49, bf16[8,16,2,2,512]{1,0,2,4,3:T(8,128)(2,1)S(1)} %broadcast_multiply_fusion), kind=kOutput, calls=%fused_computation.21 | convolution fusion | flops 1081344 | bytes 5373952 | tf_op jit(solution)/shard_map/bapk,apfk->kbpf/dot_general | solution.py:54
  38.1 3.0 %pad_maximum_fusion = f32[512,8,2,2,4]{1,4,2,0,3:T(4,128)} fusion(f32[512,8,2,1,4]{1,4,2,0,3:T(4,128)S(1)} %add_bitcast_fusion, f32[512,8,2,1,4]{1,4,2,0,3:T(4,128)S(1)} %subtract_bitcast_fusion), kind=kLoop, calls=%fused_computation.3 | loop fusion | flops 65536 | bytes 524288 | tf_op jit(solution)/shard_map/stack | solution.py:57
  41.2 3.6 %copy.53 = f32[512,8,2,2,4]{0,4,3,2,1:T(4,128)S(1)} copy(f32[512,8,2,2,4]{1,4,2,0,3:T(4,128)} %pad_maximum_fusion) | data formatting | bytes 524288 | tf_op jit(solution)/shard_map/stack | solution.py:57
  44.9 0.8 copy.54
  45.8 0.8 dynamic_slice.3
  46.5 2.5 %sort.17 = (s32[128]{0:T(128)}, s32[128]{0:T(128)S(1)}) sort(s32[128]{0:T(128)S(1)} %dynamic_slice.3, s32[128]{0:T(128)S(1)} %iota.12), dimensions={0}, to_apply=%region_0.1 | sort | flops 896 | bytes 2048 | tf_op jit(solution)/shard_map/jit(argsort)/sort | solution.py:62
  49.2 19.0 %reduce-scatter.2.cloned.1.call-done = f32[128,128]{1,0:T(8,128)} async-done(((f32[512,128]{1,0:T(8,128)}), f32[128,128]{1,0:T(8,128)}) %reduce-scatter.2.cloned.1.call-update) | async-done | bytes 65552 | tf_op jit(solution)/shard_map/reduce_scatter | solution.py:58
  68.2 0.8 convert_element_type.92
  69.0 0.7 gather_fusion
  69.8 8.4 %all_to_all.6 = bf16[8,16,128]{2,1,0:T(8,128)(2,1)S(1)} all-to-all(bf16[8,16,128]{2,1,0:T(8,128)(2,1)S(1)} %broadcast_select_fusion), channel_id=1, replica_groups=mesh['station'=8,'section'=4] {'station'}, dimensions={0} | all-to-all | bytes 65536 | tf_op jit(solution)/shard_map/all_to_all | solution.py:64
  79.4 2.5 %fusion.7 = (bf16[1,1,16,8,4,16,16]{6,5,4,3,2,1,0:T(8,128)(2,1)S(1)}, bf16[1,1,16,8,4,16,16]{6,5,4,3,2,1,0:T(8,128)(2,1)S(1)}) fusion(f32[16,8,4,16]{3,2,1,0:T(4,128)S(1)} %copy.60, f32[16,8,4,16]{3,2,1,0:T(4,128)S(1)} %copy.57), kind=kLoop, calls=%fused_computation.17 | loop fusion | flops 1048576 | bytes 589824 | tf_op jit(solution)/shard_map/concatenate | solution.py:75
  81.9 2.5 %pad_maximum_fusion.2 = bf16[1,1,16,8,4,16,32]{6,5,4,3,2,1,0:T(8,128)(2,1)} fusion(bf16[1,1,16,8,4,16,16]{6,5,4,3,2,1,0:T(8,128)(2,1)S(1)} %get-tuple-element.8, bf16[1,1,16,8,4,16,16]{6,5,4,3,2,1,0:T(8,128)(2,1)S(1)} %get-tuple-element.7), kind=kLoop, calls=%fused_computation.20 | loop fusion | flops 1048576 | bytes 1048576 | tf_op jit(solution)/shard_map/concatenate | solution.py:75
  (25 shorter events, 2.0 us)
Async XLA Ops:
  6.5 9.2 %copy-start.1 = (f32[14,1024]{1,0:T(8,128)S(1)}, f32[14,1024]{1,0:T(8,128)}, u32[]{:S(2)}) copy-start(f32[14,1024]{1,0:T(8,128)} %param.6) | copy-start | bytes 172036
  6.5 61.7 %reduce-scatter.2.cloned.1.call-start = ((), (), s32[]{:S(2)}) async-start(), calls=%async_computation.2 | async-start | bytes 327680 | tf_op jit(solution)/shard_map/reduce_scatter | solution.py:58
  20.8 1.6 %copy-start = (bf16[1,8,32,2,512]{4,3,2,1,0:T(2,128)(2,1)S(1)}, bf16[1,8,32,2,512]{4,3,2,1,0:T(2,128)(2,1)}, u32[]{:S(2)}) copy-start(bf16[1,8,32,2,512]{4,3,2,1,0:T(2,128)(2,1)} %param.7) | copy-start | bytes 1572868
  22.9 6.0 %copy-start.2 = (s32[8]{0:T(128)S(1)}, s32[8]{0:T(128)}, u32[]{:S(2)}) copy-start(s32[8]{0:T(128)} %param.8) | copy-start | bytes 100
Sparse Core Ops, SparseCore 0:
  45.9 22.2 reduce-scatter.1
where the time goes:
time: 91.6 us; the launch traced here: 91.2 us
  other arithmetic  28.3 us (31%)
  waiting for transfers between devices  19 us (21%)
  local copies, waits for them, and re-layouts  16 us (17%)
  between operations  13.6 us (15%)
  blocking collectives  8.38 us (9%)
  matrix products  5.93 us (6%)
    reduce_scatter x1, waiting for transfers between devices, local(): lax.psum_scatter(partial_sum, 'section', scatter_dimension=0, tiled=True)  19 us
    another operation x2, other arithmetic  9.27 us
    all_to_all x1, blocking collectives, local(): lax.all_to_all(placed, 'station', split_axis=0, concat_axis=0, tiled=True)  8.38 us
    convert_element_type x1, local copies, waits for them, and re-layouts, local(): beam_weight_table[0].astype(jnp.float32)  5.3 us
    concatenate x2, other arithmetic, local(): visible = jnp.concatenate([real_v, imag_v], axis=-1).astype(jnp.bfloat16)  4.97 us
    mul x1, other arithmetic, local(): scaled = scaled * inside[:, None, None, None, None]  4.13 us
    another operation x1, local copies, waits for them, and re-layouts, local(): jnp.stack([real_b, imag_b], axis=3)  3.63 us
    another operation x1, other arithmetic, local(): jnp.stack([real_b, imag_b], axis=3)  3.02 us
  transfers between devices with their start and end apart: 1, of which 1 were waited for; matrix products, arithmetic and copies ran while one was open for 4% of the time, Pallas kernels for 0%

commit v1 on v0

v1 whole, which is shorter than its diff:
```python
import functools
import math

import jax
import jax.numpy as jnp
import numpy as np
from jax import lax
from jax.experimental import pallas as pl
from jax.experimental.pallas import tpu as pltpu
from jax.sharding import PartitionSpec as P

MESH = pl.DeviceIdType.MESH
LANES = 128
F32 = jnp.float32
BF16 = jnp.bfloat16


def dft_table(length, group):
    half = length // 2
    index_n = np.arange(length, dtype=np.int64)[:, None]
    index_k = np.arange(half, dtype=np.int64)[None, :]
    phase = (index_n * index_k % length).astype(np.float32) * np.float32(2.0 * math.pi / length)
    factor = np.float32(1.0 / math.sqrt(length))
    real = (np.cos(phase) * factor).reshape(length, half // group, group)
    imag = (-np.sin(phase) * factor).reshape(length, half // group, group)
    return np.concatenate([real, imag], axis=2).transpose(1, 0, 2).astype(jnp.bfloat16)


def beam_kernel(
    dims, starts_ref, owner_ref, taper_ref, volts_hbm, weights_hbm, table_hbm, out_ref,
    volts, weights, table, filtered, spectra, outgoing, arrived, load_sems, send_sem, recv_sem,
):
    sections, stations, inputs, frames, taps, length, beams, group, block, per_owner, rows = dims
    st = lax.axis_index("station")
    sec = lax.axis_index("section")
    devices = sections * stations
    me = sec * stations + st
    groups = table.shape[0]
    group_blocks = group // block
    group_targets = group_blocks * stations

    loads = [
        pltpu.make_async_copy(volts_hbm.at[0], volts, load_sems.at[0]),
        pltpu.make_async_copy(table_hbm, table, load_sems.at[1]),
        pltpu.make_async_copy(weights_hbm, weights, load_sems.at[2]),
    ]
    for load in loads:
        load.start()

    barrier = pltpu.get_barrier_semaphore()

    def greet(step, carry):
        other = lax.rem(me + step, devices)
        pl.semaphore_signal(
            barrier, inc=1, device_id=(lax.rem(other, stations), lax.div(other, stations)),
            device_id_type=MESH,
        )
        return carry

    lax.fori_loop(1, devices, greet, 0)

    loads[0].wait()

    def filter_chunk(chunk, carry):
        at = pl.multiple_of(chunk * LANES, LANES)
        sums = [None] * frames
        for segment in range(frames + taps - 1):
            lanes = pl.ds(pl.multiple_of(segment * length + at, LANES), LANES)
            part = volts[:, lanes].astype(F32)
            for frame in range(frames):
                tap = segment - frame
                if 0 <= tap < taps:
                    term = taper_ref[tap : tap + 1, pl.ds(at, LANES)] * part
                    sums[frame] = term if sums[frame] is None else sums[frame] + term
        for frame in range(frames):
            filtered[frame * inputs : (frame + 1) * inputs, pl.ds(at, LANES)] = sums[frame].astype(BF16)
        return carry

    lax.fori_loop(0, length // LANES, filter_chunk, 0)

    beam_row = lax.broadcasted_iota(jnp.int32, (beams, group), 0)
    first = jnp.zeros((beams, group), jnp.int32)
    for beam in range(beams):
        first = jnp.where(beam_row == beam, starts_ref[beam], first)
    offset = sec - first
    offset = jnp.where(offset < 0, offset + sections, offset)
    inside = (offset < max(1, sections // 2)).astype(F32)

    def block_of(axis, shape):
        at = lax.broadcasted_iota(jnp.int32, shape, axis)
        total = jnp.zeros(shape, jnp.int32)
        for edge in range(1, group_blocks):
            total = total + (at >= edge * block).astype(jnp.int32)
        return total

    square = (group, group)
    earlier = lax.broadcasted_iota(jnp.int32, square, 0) < lax.broadcasted_iota(jnp.int32, square, 1)
    if group_blocks > 1:
        earlier = earlier & (block_of(0, square) == block_of(1, square))
    earlier = earlier.astype(F32).astype(BF16)

    loads[1].wait()
    loads[2].wait()
    pl.semaphore_wait(barrier, devices - 1)
    own_group = lax.div(sec, group_blocks)

    def one_group(step, carry):
        which = lax.rem(own_group + 1 + step, groups)
        spectra[...] = jnp.dot(filtered[...], table[which], preferred_element_type=F32)
        total = [[[None] * frames for _ in range(2)] for _ in range(2)]
        channels = pl.ds(pl.multiple_of(which * group, group), group)
        for entry in range(inputs):
            weight = weights[entry, :, channels].astype(F32)
            weight_r, weight_i = weight[:beams], weight[beams:]
            mine = total[entry % 2]
            for frame in range(frames):
                row = frame * inputs + entry
                real = spectra[row : row + 1, :group]
                imag = spectra[row : row + 1, group:]
                sum_r = weight_r * real - weight_i * imag
                sum_i = weight_r * imag + weight_i * real
                mine[0][frame] = sum_r if mine[0][frame] is None else mine[0][frame] + sum_r
                mine[1][frame] = sum_i if mine[1][frame] is None else mine[1][frame] + sum_i
        shares = jnp.concatenate(
            [total[p][part][f] * inside for p in range(2) for part in range(2) for f in range(frames)],
            axis=0,
        ).astype(BF16)
        owner = owner_ref[which]
        owned = lax.broadcasted_iota(jnp.int32, (stations, group), 0) == owner
        ahead = jnp.dot(owned.astype(F32).astype(BF16), earlier, preferred_element_type=F32)
        rank = jnp.sum(jnp.where(owned, ahead, 0.0), axis=0, keepdims=True).astype(jnp.int32)
        slot = (block_of(1, (1, group)) * stations + owner) * rows + rank
        order = lax.broadcasted_iota(jnp.int32, (group_targets * rows, group), 0) == slot
        ordered = lax.dot_general(
            order.astype(F32).astype(BF16), shares, (((1,), (1,)), ((), ())),
            preferred_element_type=F32,
        )
        base = which * group_targets
        outgoing[pl.ds(base, group_targets)] = ordered.astype(BF16).reshape(group_targets, rows, LANES)

        def send(turn, inner):
            part = lax.div(turn, stations)
            to_st = lax.rem(st + turn, stations)
            target = base + part * stations + to_st

            @pl.when(target != me)
            def _():
                pltpu.make_async_remote_copy(
                    src_ref=outgoing.at[target], dst_ref=arrived.at[me],
                    send_sem=send_sem, recv_sem=recv_sem,
                    device_id=(to_st, which * group_blocks + part), device_id_type=MESH,
                ).start()

            return inner

        lax.fori_loop(0, group_targets, send, 0)
        return carry

    lax.fori_loop(0, groups, one_group, 0)

    arrived[me] = outgoing[me]
    others = pl.ds(0, devices - 1)
    pltpu.make_async_copy(arrived.at[others], arrived.at[others], recv_sem).wait()
    summed = arrived[0:stations].astype(F32)
    for other in range(1, sections):
        summed = summed + arrived[other * stations : (other + 1) * stations].astype(F32)
    out_ref[...] = summed.astype(BF16).reshape(stations * rows, LANES)
    pltpu.make_async_copy(outgoing.at[others], outgoing.at[others], send_sem).wait()


def correlate_kernel(dims, beams_ref, place_ref, out_hbm, left, right, mask, result, sem):
    beams, frames, per_owner, signals = dims
    half = frames * beams
    spread = jnp.dot(place_ref[...], beams_ref[...], preferred_element_type=F32)
    shape = spread.shape
    lane = lax.broadcasted_iota(jnp.int32, shape, 1)
    odd = (lax.broadcasted_iota(jnp.int32, shape, 0) & 1) == 1
    both = jnp.where(odd, pltpu.roll(spread, 2 * half, 1), spread)
    turned = jnp.where(lane < half, -pltpu.roll(both, LANES - half, 1), pltpu.roll(both, half, 1))
    left[...] = both.astype(BF16).reshape(per_owner, signals, LANES)
    right[:, :signals] = left[...]
    right[:, signals:] = turned.astype(BF16).reshape(per_owner, signals, LANES)
    full = (beams, frames, signals, LANES)
    column = lax.broadcasted_iota(jnp.int32, full, 1) * beams + lax.broadcasted_iota(jnp.int32, full, 0)
    lane = lax.broadcasted_iota(jnp.int32, full, 3)
    hit = (lane == column) | (lane == column + half)
    mask[...] = hit.astype(F32).astype(BF16).reshape(half, signals, LANES)

    def channel(at, carry):
        masked = (left[at][None] * mask[...]).reshape(half * signals, LANES)
        product = lax.dot_general(
            masked, right[at], (((1,), (1,)), ((), ())), preferred_element_type=F32
        )
        result[at] = product.astype(BF16).reshape(beams, frames, signals, 2 * signals)
        pltpu.make_async_copy(result.at[at], out_hbm.at[0, 0, at], sem).start()
        return carry

    lax.fori_loop(0, per_owner, channel, 0)
    pltpu.make_async_copy(result, out_hbm.at[0, 0], sem).wait()


def local(voltages, taper, beam_weight_table, starts, owner_map):
    inputs = voltages.shape[1]
    taps, length = taper.shape
    frames = voltages.shape[2] // length - taps + 1
    channels = length // 2
    beams = beam_weight_table.shape[1]
    sections = lax.axis_size("section")
    stations = lax.axis_size("station")
    block = channels // sections
    per_owner = block // stations
    group = max(LANES, block)
    groups = channels // group
    rows = -(-per_owner // 16) * 16
    devices = sections * stations
    signals = 2 * stations
    values = 4 * frames * beams
    dims = (sections, stations, inputs, frames, taps, length, beams, group, block, per_owner, rows)

    weights = jnp.transpose(beam_weight_table[0], (1, 2, 0, 3)).reshape(inputs, 2 * beams, channels)
    table = jnp.asarray(dft_table(length, group))
    owners = owner_map.reshape(groups, 1, group)
    vmem = pl.BlockSpec(memory_space=pltpu.VMEM)
    hbm = pl.BlockSpec(memory_space=pl.ANY)
    mine = pl.pallas_call(
        functools.partial(beam_kernel, dims),
        out_shape=jax.ShapeDtypeStruct((stations * rows, values), BF16),
        in_specs=[pl.BlockSpec(memory_space=pltpu.SMEM), vmem, vmem, hbm, hbm, hbm],
        out_specs=vmem,
        scratch_shapes=[
            pltpu.VMEM(voltages.shape[1:], BF16),
            pltpu.VMEM(weights.shape, BF16),
            pltpu.VMEM(table.shape, BF16),
            pltpu.VMEM((frames * inputs, length), BF16),
            pltpu.VMEM((frames * inputs, 2 * group), F32),
            pltpu.VMEM((devices, rows, values), BF16),
            pltpu.VMEM((devices, rows, values), BF16),
            pltpu.SemaphoreType.DMA((3,)),
            pltpu.SemaphoreType.DMA,
            pltpu.SemaphoreType.DMA,
        ],
        compiler_params=pltpu.CompilerParams(
            collective_id=0, has_side_effects=True, vmem_limit_bytes=40 * 1024 * 1024
        ),
    )(starts, owners, taper, voltages, weights, table)

    place = np.zeros((per_owner, stations, 2, stations, rows), np.float32)
    for at in range(per_owner):
        for station in range(stations):
            place[at, station, :, station, at] = 1.0
    place = jnp.asarray(place.reshape(per_owner * signals, stations * rows).astype(jnp.bfloat16))
    return pl.pallas_call(
        functools.partial(correlate_kernel, (beams, frames, per_owner, signals)),
        out_shape=jax.ShapeDtypeStruct(
            (1, 1, per_owner, beams, frames, signals, 2 * signals), BF16
        ),
        in_specs=[vmem, vmem],
        out_specs=hbm,
        scratch_shapes=[
            pltpu.VMEM((per_owner, signals, LANES), BF16),
            pltpu.VMEM((per_owner, 2 * signals, LANES), BF16),
            pltpu.VMEM((frames * beams, signals, LANES), BF16),
            pltpu.VMEM((per_owner, beams, frames, signals, 2 * signals), BF16),
            pltpu.SemaphoreType.DMA,
        ],
        compiler_params=pltpu.CompilerParams(vmem_limit_bytes=40 * 1024 * 1024),
    )(mine, place)


def solution(mesh):
    placed = (
        P("station", "section", None),
        P(),
        P("station", None, "section", None, None),
        P(),
        P(),
    )
    return jax.shard_map(
        local,
        mesh=mesh,
        in_specs=placed,
        out_specs=P("section", "station", None, None, None, None, None),
        check_vma=False,
    )
```

time: 91.6 us -> 23.5 us (0.26)
  other arithmetic: 28.3 us -> 0 us
  waiting for transfers between devices: 19 us -> 0 us
  Pallas kernels: 0 us -> 16.6 us
  between operations: 13.6 us -> 0.03 us
  local copies, waits for them, and re-layouts: 16 us -> 6.49 us
  blocking collectives: 8.38 us -> 0 us
  matrix products: 5.93 us -> 0 us
    reduce_scatter x1 -> x0, waiting for transfers between devices: 19 us -> none  [local(): lax.psum_scatter(partial_sum, 'section', scatter_dimension=0, tiled=True)]
    pallas_call x0 -> x2, Pallas kernels: none -> 16.6 us  [the longest x1 12.9 us: local(): pl.pallas_call(functools.partial(beam_kernel, dims), out_shape=jax.ShapeD...]
    another operation x3 -> x0, other arithmetic: 12.3 us -> none
    all_to_all x1 -> x0, blocking collectives: 8.38 us -> none  [local(): lax.all_to_all(placed, 'station', split_axis=0, concat_axis=0, tiled=True)]
    concatenate x3 -> x0, other arithmetic: 6.37 us -> none  [the longest x2 4.97 us: local(): visible = jnp.concatenate([real_v, imag_v], axis=-1).astype(jnp.bfloat16)]
    another operation x6 -> x0, local copies, waits for them, and re-layouts: 6.2 us -> none  [the longest x1 3.63 us: local(): jnp.stack([real_b, imag_b], axis=3)]
    dot_general x5 -> x0, matrix products: 5.93 us -> none  [the longest x1 1.28 us: local(): jnp.einsum('bapk,apfk->kbpf', real_w, imag_x)]
    convert_element_type x1 -> x0, local copies, waits for them, and re-layouts: 5.3 us -> none  [local(): beam_weight_table[0].astype(jnp.float32)]
  transfers between devices with their start and end apart: 1 -> 0, of which waited for: 1 -> 0; matrix products, arithmetic and copies ran while one was open for 4% -> 0% of each run, Pallas kernels for 0% -> 0%
where the time goes in v1:
time: 23.5 us; the launch traced here: 23.2 us
  Pallas kernels  16.6 us (71%)
  local copies, waits for them, and re-layouts  6.49 us (28%)
    pallas_call x1, Pallas kernels, local(): pl.pallas_call(functools.partial(beam_kernel, dims), out_shape=jax.ShapeD...  12.9 us
    unnamed x12, local copies, waits for them, and re-layouts  5.01 us
    pallas_call x1, Pallas kernels, local(): pl.pallas_call(functools.partial(correlate_kernel, (beams, frames, per_ow...  3.7 us
    transpose x1, local copies, waits for them, and re-layouts, local(): jnp.transpose(beam_weight_table[0], (1, 2, 0, 3))  1.48 us

profile of v1, /device:TPU:0, one launch (start us, length us, event | category | flops | bytes accessed | tf_op | source)
XLA Modules:
  0.0 23.2 jit_solution(1339463527979130108)
XLA Ops:
  0.0 1.5 %copy.10 = bf16[32,2,8,512]{3,2,1,0:T(8,128)(2,1)S(1)} copy(bf16[32,2,8,512]{3,1,0,2:T(2,128)(2,1)} %bitcast.9) | data formatting | bytes 1048576 | tf_op jit(solution)/shard_map/transpose | solution.py:220
  1.5 0.0 copy-start
  1.5 1.6 %copy-done = bf16[4,1024,256]{2,1,0:T(8,128)(2,1)S(1)} copy-done((bf16[4,1024,256]{2,1,0:T(8,128)(2,1)S(1)}, bf16[4,1024,256]{2,1,0:T(8,128)(2,1)}, u32[]{:S(2)}) %copy-start) | copy-done | bytes 2097176
  3.1 0.0 copy-start.1
  3.1 1.2 %copy-done.1 = bf16[1,32,17408]{2,1,0:T(8,128)(2,1)S(1)} copy-done((bf16[1,32,17408]{2,1,0:T(8,128)(2,1)S(1)}, bf16[1,32,17408]{2,1,0:T(8,128)(2,1)}, u32[]{:S(2)}) %copy-start.1) | copy-done | bytes 1114136
  4.3 0.0 copy-start.2
  4.3 0.8 %copy-done.2 = f32[14,1024]{1,0:T(8,128)S(1)} copy-done((f32[14,1024]{1,0:T(8,128)S(1)}, f32[14,1024]{1,0:T(8,128)}, u32[]{:S(2)}) %copy-start.2) | copy-done | bytes 57368
  5.2 0.0 copy-start.4
  5.2 0.7 %copy-done.4 = s32[512]{0:T(512)S(1)} copy-done((s32[512]{0:T(512)S(1)}, s32[512]{0:T(512)}, u32[]{:S(2)}) %copy-start.4) | copy-done | bytes 2072
  5.8 0.0 copy-start.5
  5.8 0.7 %copy-done.5 = s32[8]{0:T(128)S(1)} copy-done((s32[8]{0:T(128)S(1)}, s32[8]{0:T(128)}, u32[]{:S(2)}) %copy-start.5) | copy-done | bytes 56
  6.5 0.0 copy-start.3
  6.5 12.9 %shard_map.73.beams_ref = bf16[128,128]{1,0:T(8,128)(2,1)S(1)} custom-call(s32[8]{0:T(128)S(1)} %copy-done.5, s32[4,1,128]{2,1,0:T(1,128)S(1)} %bitcast.8, f32[14,1024]{1,0:T(8,128)S(1)} %copy-done.2, bf16[1,32,17408]{2,1,0:T(8,128)(2,1)S(1)} %copy-done.1, bf16[32,16,512]{2,1,0:T(8,128)(2,1)S(1)} %bitcast.7, bf16[4,1024,256]{2,1,0:T(8,128)(2,1)S(1)} %copy-done), custom_call_target="tpu_custom_call" | custom-call | tf_op jit(solution)/shard_map/pallas_call | solution.py:225
  19.5 0.0 copy-done.3
  19.5 3.7 %shard_map.74 = bf16[1,1,16,8,4,16,32]{6,5,4,3,2,1,0:T(8,128)(2,1)} custom-call(bf16[128,128]{1,0:T(8,128)(2,1)S(1)} %shard_map.73.beams_ref, bf16[256,128]{1,0:T(8,128)(2,1)S(1)} %copy-done.3), custom_call_target="tpu_custom_call" | custom-call | tf_op jit(solution)/shard_map/pallas_call | solution.py:252
Async XLA Ops:
  1.5 1.6 %copy-start = (bf16[4,1024,256]{2,1,0:T(8,128)(2,1)S(1)}, bf16[4,1024,256]{2,1,0:T(8,128)(2,1)}, u32[]{:S(2)}) copy-start(bf16[4,1024,256]{2,1,0:T(8,128)(2,1)} %constant.4.clone.table_hbm) | copy-start | bytes 6291460
  3.1 1.2 %copy-start.1 = (bf16[1,32,17408]{2,1,0:T(8,128)(2,1)S(1)}, bf16[1,32,17408]{2,1,0:T(8,128)(2,1)}, u32[]{:S(2)}) copy-start(bf16[1,32,17408]{2,1,0:T(8,128)(2,1)} %volts_hbm.1) | copy-start | bytes 3342340
  4.3 0.8 %copy-start.2 = (f32[14,1024]{1,0:T(8,128)S(1)}, f32[14,1024]{1,0:T(8,128)}, u32[]{:S(2)}) copy-start(f32[14,1024]{1,0:T(8,128)} %taper_ref.1) | copy-start | bytes 172036
  5.2 0.7 %copy-start.4 = (s32[512]{0:T(512)S(1)}, s32[512]{0:T(512)}, u32[]{:S(2)}) copy-start(s32[512]{0:T(512)} %param.11) | copy-start | bytes 6148
  5.8 0.7 %copy-start.5 = (s32[8]{0:T(128)S(1)}, s32[8]{0:T(128)}, u32[]{:S(2)}) copy-start(s32[8]{0:T(128)} %starts_ref.1) | copy-start | bytes 100
  6.5 13.0 %copy-start.3 = (bf16[256,128]{1,0:T(8,128)(2,1)S(1)}, bf16[256,128]{1,0:T(8,128)(2,1)}, u32[]{:S(2)}) copy-start(bf16[256,128]{1,0:T(8,128)(2,1)} %constant.5.clone.place_ref) | copy-start | bytes 196612

commit v2 on v1

--- a/solution.py
+++ b/solution.py
@@ -11,6 +11,7 @@
 
 MESH = pl.DeviceIdType.MESH
 LANES = 128
+VMEM_LIMIT = 60 * 1024 * 1024
 F32 = jnp.float32
 BF16 = jnp.bfloat16
 
@@ -27,8 +28,9 @@
 
 
 def beam_kernel(
-    dims, starts_ref, owner_ref, taper_ref, volts_hbm, weights_hbm, table_hbm, out_ref,
-    volts, weights, table, filtered, spectra, outgoing, arrived, load_sems, send_sem, recv_sem,
+    dims, starts_hbm, owner_hbm, taper_hbm, volts_hbm, weights_hbm, table_hbm, out_ref,
+    starts_ref, owner_ref, taper_ref, volts, weights, table, filtered, spectra_a, spectra_b, orders,
+    outgoing, arrived, load_sems, send_sem, recv_sem,
 ):
     sections, stations, inputs, frames, taps, length, beams, group, block, per_owner, rows = dims
     st = lax.axis_index("station")
@@ -39,10 +41,14 @@
     group_blocks = group // block
     group_targets = group_blocks * stations
 
+    own_group = lax.div(sec, group_blocks)
+    turns = [lax.rem(own_group + 1 + step, groups) for step in range(groups)]
+    pairs = [(volts_hbm.at[0], volts), (taper_hbm, taper_ref), (owner_hbm, owner_ref), (starts_hbm, starts_ref)]
+    pairs += [(table_hbm.at[turn], table.at[turn]) for turn in turns[:1]]
+    pairs += [(weights_hbm, weights)]
+    pairs += [(table_hbm.at[turn], table.at[turn]) for turn in turns[1:]]
     loads = [
-        pltpu.make_async_copy(volts_hbm.at[0], volts, load_sems.at[0]),
-        pltpu.make_async_copy(table_hbm, table, load_sems.at[1]),
-        pltpu.make_async_copy(weights_hbm, weights, load_sems.at[2]),
+        pltpu.make_async_copy(here, there, load_sems.at[at]) for at, (here, there) in enumerate(pairs)
     ]
     for load in loads:
         load.start()
@@ -59,7 +65,35 @@
 
     lax.fori_loop(1, devices, greet, 0)
 
+    def block_of(axis, shape):
+        at = lax.broadcasted_iota(jnp.int32, shape, axis)
+        total = jnp.zeros(shape, jnp.int32)
+        for edge in range(1, group_blocks):
+            total = total + (at >= edge * block).astype(jnp.int32)
+        return total
+
+    square = (group, group)
+    earlier = lax.broadcasted_iota(jnp.int32, square, 0) < lax.broadcasted_iota(jnp.int32, square, 1)
+    if group_blocks > 1:
+        earlier = earlier & (block_of(0, square) == block_of(1, square))
+    earlier = earlier.astype(F32).astype(BF16)
+
+    loads[2].wait()
+
+    def make_order(which, carry):
+        owner = owner_ref[which]
+        owned = lax.broadcasted_iota(jnp.int32, (stations, group), 0) == owner
+        ahead = jnp.dot(owned.astype(F32).astype(BF16), earlier, preferred_element_type=F32)
+        rank = jnp.sum(jnp.where(owned, ahead, 0.0), axis=0, keepdims=True).astype(jnp.int32)
+        slot = (block_of(1, (1, group)) * stations + owner) * rows + rank
+        order = lax.broadcasted_iota(jnp.int32, (group_targets * rows, group), 0) == slot
+        orders[which] = order.astype(F32).astype(BF16)
+        return carry
+
+    lax.fori_loop(0, groups, make_order, 0)
+
     loads[0].wait()
+    loads[1].wait()
 
     def filter_chunk(chunk, carry):
         at = pl.multiple_of(chunk * LANES, LANES)
@@ -78,6 +112,7 @@
 
     lax.fori_loop(0, length // LANES, filter_chunk, 0)
 
+    loads[3].wait()
     beam_row = lax.broadcasted_iota(jnp.int32, (beams, group), 0)
     first = jnp.zeros((beams, group), jnp.int32)
     for beam in range(beams):
@@ -86,27 +121,21 @@
     offset = jnp.where(offset < 0, offset + sections, offset)
     inside = (offset < max(1, sections // 2)).astype(F32)
 
-    def block_of(axis, shape):
-        at = lax.broadcasted_iota(jnp.int32, shape, axis)
-        total = jnp.zeros(shape, jnp.int32)
-        for edge in range(1, group_blocks):
-            total = total + (at >= edge * block).astype(jnp.int32)
-        return total
-
-    square = (group, group)
-    earlier = lax.broadcasted_iota(jnp.int32, square, 0) < lax.broadcasted_iota(jnp.int32, square, 1)
-    if group_blocks > 1:
-        earlier = earlier & (block_of(0, square) == block_of(1, square))
-    earlier = earlier.astype(F32).astype(BF16)
-
-    loads[1].wait()
-    loads[2].wait()
+    def transform(step):
+        target = (spectra_a, spectra_b)[step % 2]
+        target[...] = jnp.dot(filtered[...], table[turns[step]], preferred_element_type=F32)
+
+    loads[4].wait()
+    transform(0)
+    loads[5].wait()
     pl.semaphore_wait(barrier, devices - 1)
-    own_group = lax.div(sec, group_blocks)
-
-    def one_group(step, carry):
-        which = lax.rem(own_group + 1 + step, groups)
-        spectra[...] = jnp.dot(filtered[...], table[which], preferred_element_type=F32)
+
+    for step in range(groups):
+        which = turns[step]
+        spectra = (spectra_a, spectra_b)[step % 2]
+        if step + 1 < groups:
+            loads[6 + step].wait()
+            transform(step + 1)
         total = [[[None] * frames for _ in range(2)] for _ in range(2)]
         channels = pl.ds(pl.multiple_of(which * group, group), group)
         for entry in range(inputs):
@@ -125,20 +154,13 @@
             [total[p][part][f] * inside for p in range(2) for part in range(2) for f in range(frames)],
             axis=0,
         ).astype(BF16)
-        owner = owner_ref[which]
-        owned = lax.broadcasted_iota(jnp.int32, (stations, group), 0) == owner
-        ahead = jnp.dot(owned.astype(F32).astype(BF16), earlier, preferred_element_type=F32)
-        rank = jnp.sum(jnp.where(owned, ahead, 0.0), axis=0, keepdims=True).astype(jnp.int32)
-        slot = (block_of(1, (1, group)) * stations + owner) * rows + rank
-        order = lax.broadcasted_iota(jnp.int32, (group_targets * rows, group), 0) == slot
         ordered = lax.dot_general(
-            order.astype(F32).astype(BF16), shares, (((1,), (1,)), ((), ())),
-            preferred_element_type=F32,
+            orders[which], shares, (((1,), (1,)), ((), ())), preferred_element_type=F32
         )
         base = which * group_targets
         outgoing[pl.ds(base, group_targets)] = ordered.astype(BF16).reshape(group_targets, rows, LANES)
 
-        def send(turn, inner):
+        def send(turn, carry):
             part = lax.div(turn, stations)
             to_st = lax.rem(st + turn, stations)
             target = base + part * stations + to_st
@@ -151,12 +173,9 @@
                     device_id=(to_st, which * group_blocks + part), device_id_type=MESH,
                 ).start()
 
-            return inner
+            return carry
 
         lax.fori_loop(0, group_targets, send, 0)
-        return carry
-
-    lax.fori_loop(0, groups, one_group, 0)
 
     arrived[me] = outgoing[me]
     others = pl.ds(0, devices - 1)
@@ -186,16 +205,25 @@
     hit = (lane == column) | (lane == column + half)
     mask[...] = hit.astype(F32).astype(BF16).reshape(half, signals, LANES)
 
-    def channel(at, carry):
-        masked = (left[at][None] * mask[...]).reshape(half * signals, LANES)
-        product = lax.dot_general(
-            masked, right[at], (((1,), (1,)), ((), ())), preferred_element_type=F32
-        )
-        result[at] = product.astype(BF16).reshape(beams, frames, signals, 2 * signals)
-        pltpu.make_async_copy(result.at[at], out_hbm.at[0, 0, at], sem).start()
+    batch = math.gcd(4, per_owner)
+
+    def channels(step, carry):
+        first = step * batch
+        products = []
+        for at in range(batch):
+            masked = (left[first + at][None] * mask[...]).reshape(half * signals, LANES)
+            products.append(
+                lax.dot_general(
+                    masked, right[first + at], (((1,), (1,)), ((), ())), preferred_element_type=F32
+                )
+            )
+        for at in range(batch):
+            result[first + at] = products[at].astype(BF16).reshape(beams, frames, signals, 2 * signals)
+        several = pl.ds(first, batch)
+        pltpu.make_async_copy(result.at[several], out_hbm.at[0, 0, several], sem).start()
         return carry
 
-    lax.fori_loop(0, per_owner, channel, 0)
+    lax.fori_loop(0, per_owner // batch, channels, 0)
     pltpu.make_async_copy(result, out_hbm.at[0, 0], sem).wait()
 
 
@@ -225,22 +253,27 @@
     mine = pl.pallas_call(
         functools.partial(beam_kernel, dims),
         out_shape=jax.ShapeDtypeStruct((stations * rows, values), BF16),
-        in_specs=[pl.BlockSpec(memory_space=pltpu.SMEM), vmem, vmem, hbm, hbm, hbm],
+        in_specs=[hbm] * 6,
         out_specs=vmem,
         scratch_shapes=[
+            pltpu.SMEM(starts.shape, jnp.int32),
+            pltpu.VMEM(owners.shape, jnp.int32),
+            pltpu.VMEM(taper.shape, F32),
             pltpu.VMEM(voltages.shape[1:], BF16),
             pltpu.VMEM(weights.shape, BF16),
             pltpu.VMEM(table.shape, BF16),
             pltpu.VMEM((frames * inputs, length), BF16),
             pltpu.VMEM((frames * inputs, 2 * group), F32),
+            pltpu.VMEM((frames * inputs, 2 * group), F32),
+            pltpu.VMEM((groups, group // per_owner * rows, group), BF16),
             pltpu.VMEM((devices, rows, values), BF16),
             pltpu.VMEM((devices, rows, values), BF16),
-            pltpu.SemaphoreType.DMA((3,)),
+            pltpu.SemaphoreType.DMA((5 + groups,)),
             pltpu.SemaphoreType.DMA,
             pltpu.SemaphoreType.DMA,
         ],
         compiler_params=pltpu.CompilerParams(
-            collective_id=0, has_side_effects=True, vmem_limit_bytes=40 * 1024 * 1024
+            collective_id=0, has_side_effects=True, vmem_limit_bytes=VMEM_LIMIT
         ),
     )(starts, owners, taper, voltages, weights, table)
 
@@ -263,7 +296,7 @@
             pltpu.VMEM((per_owner, beams, frames, signals, 2 * signals), BF16),
             pltpu.SemaphoreType.DMA,
         ],
-        compiler_params=pltpu.CompilerParams(vmem_limit_bytes=40 * 1024 * 1024),
+        compiler_params=pltpu.CompilerParams(vmem_limit_bytes=32 * 1024 * 1024),
     )(mine, place)
 
 

time: 23.5 us -> 18.3 us (0.78)
  local copies, waits for them, and re-layouts: 6.49 us -> 3.03 us
  Pallas kernels: 16.6 us -> 15.1 us
    unnamed x12 -> x4, local copies, waits for them, and re-layouts: 5.01 us -> 0.75 us
    pallas_call x1, Pallas kernels: 3.7 us -> 2.28 us  [local(): pl.pallas_call(functools.partial(correlate_kernel, (beams, frames, per_ow...]
    transpose x1, local copies, waits for them, and re-layouts: 1.48 us -> 2.27 us  [local(): jnp.transpose(beam_weight_table[0], (1, 2, 0, 3))]
where the time goes in v2:
time: 18.3 us; the launch traced here: 18.1 us
  Pallas kernels  15.1 us (83%)
  local copies, waits for them, and re-layouts  3.03 us (17%)
    pallas_call x1, Pallas kernels, local(): pl.pallas_call(functools.partial(beam_kernel, dims), out_shape=jax.ShapeD...  12.8 us
    pallas_call x1, Pallas kernels, local(): pl.pallas_call(functools.partial(correlate_kernel, (beams, frames, per_ow...  2.28 us
    transpose x1, local copies, waits for them, and re-layouts, local(): jnp.transpose(beam_weight_table[0], (1, 2, 0, 3))  2.27 us
    unnamed x4, local copies, waits for them, and re-layouts  0.75 us

profile of v2, /device:TPU:0, one launch (start us, length us, event | category | flops | bytes accessed | tf_op | source)
XLA Modules:
  0.0 18.1 jit_solution(1521153207666591240)
XLA Ops:
  0.0 2.3 %copy.10 = bf16[32,2,8,512]{3,2,1,0:T(8,128)(2,1)} copy(bf16[32,2,8,512]{3,1,0,2:T(2,128)(2,1)} %bitcast.8) | data formatting | bytes 1048576 | tf_op jit(solution)/shard_map/transpose | solution.py:248
  2.3 0.0 copy-start.1
  2.3 12.8 %shard_map.73.beams_ref = bf16[128,128]{1,0:T(8,128)(2,1)} custom-call(s32[8]{0:T(128)} %starts_hbm.1, s32[4,1,128]{2,1,0:T(1,128)} %bitcast.9, f32[14,1024]{1,0:T(8,128)} %taper_hbm.1, bf16[1,32,17408]{2,1,0:T(8,128)(2,1)} %volts_hbm.1, bf16[32,16,512]{2,1,0:T(8,128)(2,1)} %bitcast.7, bf16[4,1024,256]{2,1,0:T(8,128)(2,1)} %constant.4.clone.table_hbm), custom_call_target="tpu_custom_call" | custom-call | tf_op jit(solution)/shard_map/pallas_call | solution.py:253
  15.1 0.0 copy-done.1
  15.1 0.0 copy-start
  15.1 0.7 %copy-done = bf16[128,128]{1,0:T(8,128)(2,1)S(1)} copy-done((bf16[128,128]{1,0:T(8,128)(2,1)S(1)}, bf16[128,128]{1,0:T(8,128)(2,1)}, u32[]{:S(2)}) %copy-start) | copy-done | bytes 32792
  15.8 2.3 %shard_map.74 = bf16[1,1,16,8,4,16,32]{6,5,4,3,2,1,0:T(8,128)(2,1)} custom-call(bf16[128,128]{1,0:T(8,128)(2,1)S(1)} %copy-done, bf16[256,128]{1,0:T(8,128)(2,1)S(1)} %copy-done.1), custom_call_target="tpu_custom_call" | custom-call | tf_op jit(solution)/shard_map/pallas_call | solution.py:285
Async XLA Ops:
  2.3 12.8 %copy-start.1 = (bf16[256,128]{1,0:T(8,128)(2,1)S(1)}, bf16[256,128]{1,0:T(8,128)(2,1)}, u32[]{:S(2)}) copy-start(bf16[256,128]{1,0:T(8,128)(2,1)} %constant.5.clone.place_ref) | copy-start | bytes 196612
  15.1 0.8 %copy-start = (bf16[128,128]{1,0:T(8,128)(2,1)S(1)}, bf16[128,128]{1,0:T(8,128)(2,1)}, u32[]{:S(2)}) copy-start(bf16[128,128]{1,0:T(8,128)(2,1)} %shard_map.73.beams_ref) | copy-start | bytes 98308

commit v3 on v2

--- a/solution.py
+++ b/solution.py
@@ -29,7 +29,7 @@
 
 def beam_kernel(
     dims, starts_hbm, owner_hbm, taper_hbm, volts_hbm, weights_hbm, table_hbm, out_ref,
-    starts_ref, owner_ref, taper_ref, volts, weights, table, filtered, spectra_a, spectra_b, orders,
+    starts_ref, owner_ref, taper_ref, volts, weights, wide, table, filtered, spectra_a, spectra_b, orders,
     outgoing, arrived, load_sems, send_sem, recv_sem,
 ):
     sections, stations, inputs, frames, taps, length, beams, group, block, per_owner, rows = dims
@@ -43,10 +43,11 @@
 
     own_group = lax.div(sec, group_blocks)
     turns = [lax.rem(own_group + 1 + step, groups) for step in range(groups)]
-    pairs = [(volts_hbm.at[0], volts), (taper_hbm, taper_ref), (owner_hbm, owner_ref), (starts_hbm, starts_ref)]
-    pairs += [(table_hbm.at[turn], table.at[turn]) for turn in turns[:1]]
-    pairs += [(weights_hbm, weights)]
-    pairs += [(table_hbm.at[turn], table.at[turn]) for turn in turns[1:]]
+    pairs = [
+        (owner_hbm, owner_ref), (weights_hbm.at[0], weights), (volts_hbm.at[0], volts),
+        (taper_hbm, taper_ref), (starts_hbm, starts_ref),
+    ]
+    pairs += [(table_hbm.at[turn], table.at[turn]) for turn in turns]
     loads = [
         pltpu.make_async_copy(here, there, load_sems.at[at]) for at, (here, there) in enumerate(pairs)
     ]
@@ -78,7 +79,7 @@
         earlier = earlier & (block_of(0, square) == block_of(1, square))
     earlier = earlier.astype(F32).astype(BF16)
 
-    loads[2].wait()
+    loads[0].wait()
 
     def make_order(which, carry):
         owner = owner_ref[which]
@@ -92,8 +93,20 @@
 
     lax.fori_loop(0, groups, make_order, 0)
 
-    loads[0].wait()
     loads[1].wait()
+    few = 4
+
+    def widen(step, carry):
+        beam, at = lax.div(step, inputs // few), lax.rem(step, inputs // few)
+        part = weights[beam, pl.ds(at * few, few)].astype(F32).reshape(2 * few, groups * group)
+        for which in range(groups):
+            wide[which, pl.ds(step * 2 * few, 2 * few), :] = part[:, which * group : (which + 1) * group]
+        return carry
+
+    lax.fori_loop(0, beams * inputs // few, widen, 0, unroll=4)
+
+    loads[2].wait()
+    loads[3].wait()
 
     def filter_chunk(chunk, carry):
         at = pl.multiple_of(chunk * LANES, LANES)
@@ -112,7 +125,7 @@
 
     lax.fori_loop(0, length // LANES, filter_chunk, 0)
 
-    loads[3].wait()
+    loads[4].wait()
     beam_row = lax.broadcasted_iota(jnp.int32, (beams, group), 0)
     first = jnp.zeros((beams, group), jnp.int32)
     for beam in range(beams):
@@ -125,9 +138,8 @@
         target = (spectra_a, spectra_b)[step % 2]
         target[...] = jnp.dot(filtered[...], table[turns[step]], preferred_element_type=F32)
 
-    loads[4].wait()
+    loads[5].wait()
     transform(0)
-    loads[5].wait()
     pl.semaphore_wait(barrier, devices - 1)
 
     for step in range(groups):
@@ -137,10 +149,9 @@
             loads[6 + step].wait()
             transform(step + 1)
         total = [[[None] * frames for _ in range(2)] for _ in range(2)]
-        channels = pl.ds(pl.multiple_of(which * group, group), group)
         for entry in range(inputs):
-            weight = weights[entry, :, channels].astype(F32)
-            weight_r, weight_i = weight[:beams], weight[beams:]
+            weight_r = wide[which, pl.ds(2 * entry, beams, stride=2 * inputs), :]
+            weight_i = wide[which, pl.ds(2 * entry + 1, beams, stride=2 * inputs), :]
             mine = total[entry % 2]
             for frame in range(frames):
                 row = frame * inputs + entry
@@ -187,9 +198,24 @@
     pltpu.make_async_copy(outgoing.at[others], outgoing.at[others], send_sem).wait()
 
 
-def correlate_kernel(dims, beams_ref, place_ref, out_hbm, left, right, mask, result, sem):
+def correlate_kernel(
+    dims, beams_hbm, place_hbm, out_hbm, beams_ref, place_ref, left, right, mask, result, sems, sem
+):
     beams, frames, per_owner, signals = dims
     half = frames * beams
+    loads = [
+        pltpu.make_async_copy(beams_hbm, beams_ref, sems.at[0]),
+        pltpu.make_async_copy(place_hbm, place_ref, sems.at[1]),
+    ]
+    for load in loads:
+        load.start()
+    full = (beams, frames, signals, LANES)
+    column = lax.broadcasted_iota(jnp.int32, full, 1) * beams + lax.broadcasted_iota(jnp.int32, full, 0)
+    lane = lax.broadcasted_iota(jnp.int32, full, 3)
+    hit = (lane == column) | (lane == column + half)
+    mask[...] = hit.astype(F32).astype(BF16).reshape(half, signals, LANES)
+    for load in loads:
+        load.wait()
     spread = jnp.dot(place_ref[...], beams_ref[...], preferred_element_type=F32)
     shape = spread.shape
     lane = lax.broadcasted_iota(jnp.int32, shape, 1)
@@ -199,11 +225,6 @@
     left[...] = both.astype(BF16).reshape(per_owner, signals, LANES)
     right[:, :signals] = left[...]
     right[:, signals:] = turned.astype(BF16).reshape(per_owner, signals, LANES)
-    full = (beams, frames, signals, LANES)
-    column = lax.broadcasted_iota(jnp.int32, full, 1) * beams + lax.broadcasted_iota(jnp.int32, full, 0)
-    lane = lax.broadcasted_iota(jnp.int32, full, 3)
-    hit = (lane == column) | (lane == column + half)
-    mask[...] = hit.astype(F32).astype(BF16).reshape(half, signals, LANES)
 
     batch = math.gcd(4, per_owner)
 
@@ -245,7 +266,6 @@
     values = 4 * frames * beams
     dims = (sections, stations, inputs, frames, taps, length, beams, group, block, per_owner, rows)
 
-    weights = jnp.transpose(beam_weight_table[0], (1, 2, 0, 3)).reshape(inputs, 2 * beams, channels)
     table = jnp.asarray(dft_table(length, group))
     owners = owner_map.reshape(groups, 1, group)
     vmem = pl.BlockSpec(memory_space=pltpu.VMEM)
@@ -260,7 +280,8 @@
             pltpu.VMEM(owners.shape, jnp.int32),
             pltpu.VMEM(taper.shape, F32),
             pltpu.VMEM(voltages.shape[1:], BF16),
-            pltpu.VMEM(weights.shape, BF16),
+            pltpu.VMEM(beam_weight_table.shape[1:], BF16),
+            pltpu.VMEM((groups, 2 * beams * inputs, group), F32),
             pltpu.VMEM(table.shape, BF16),
             pltpu.VMEM((frames * inputs, length), BF16),
             pltpu.VMEM((frames * inputs, 2 * group), F32),
@@ -275,7 +296,7 @@
         compiler_params=pltpu.CompilerParams(
             collective_id=0, has_side_effects=True, vmem_limit_bytes=VMEM_LIMIT
         ),
-    )(starts, owners, taper, voltages, weights, table)
+    )(starts, owners, taper, voltages, beam_weight_table, table)
 
     place = np.zeros((per_owner, stations, 2, stations, rows), np.float32)
     for at in range(per_owner):
@@ -287,16 +308,19 @@
         out_shape=jax.ShapeDtypeStruct(
             (1, 1, per_owner, beams, frames, signals, 2 * signals), BF16
         ),
-        in_specs=[vmem, vmem],
+        in_specs=[hbm, hbm],
         out_specs=hbm,
         scratch_shapes=[
+            pltpu.VMEM(mine.shape, BF16),
+            pltpu.VMEM(place.shape, BF16),
             pltpu.VMEM((per_owner, signals, LANES), BF16),
             pltpu.VMEM((per_owner, 2 * signals, LANES), BF16),
             pltpu.VMEM((frames * beams, signals, LANES), BF16),
             pltpu.VMEM((per_owner, beams, frames, signals, 2 * signals), BF16),
+            pltpu.SemaphoreType.DMA((2,)),
             pltpu.SemaphoreType.DMA,
         ],
-        compiler_params=pltpu.CompilerParams(vmem_limit_bytes=32 * 1024 * 1024),
+        compiler_params=pltpu.CompilerParams(vmem_limit_bytes=VMEM_LIMIT),
     )(mine, place)
 
 

time: 18.3 us -> 16.2 us (0.89)
  local copies, waits for them, and re-layouts: 3.03 us -> 0 us
  Pallas kernels: 15.1 us -> 16.1 us
    transpose x1 -> x0, local copies, waits for them, and re-layouts: 2.27 us -> none  [local(): jnp.transpose(beam_weight_table[0], (1, 2, 0, 3))]
    pallas_call x1, Pallas kernels: 2.28 us -> 3.16 us  [local(): pl.pallas_call(functools.partial(correlate_kernel, (beams, frames, per_ow...]
    unnamed x4 -> x0, local copies, waits for them, and re-layouts: 0.75 us -> none
where the time goes in v3:
time: 16.2 us; the launch traced here: 16.1 us
  Pallas kernels  16.1 us (99%)
    pallas_call x1, Pallas kernels, local(): pl.pallas_call(functools.partial(beam_kernel, dims), out_shape=jax.ShapeD...  12.9 us
    pallas_call x1, Pallas kernels, local(): pl.pallas_call(functools.partial(correlate_kernel, (beams, frames, per_ow...  3.16 us

profile of v3, /device:TPU:0, one launch (start us, length us, event | category | flops | bytes accessed | tf_op | source)
XLA Modules:
  0.0 16.1 jit_solution(11977134934737552025)
XLA Ops:
  0.0 12.9 %shard_map.73.beams_hbm = bf16[128,128]{1,0:T(8,128)(2,1)} custom-call(s32[8]{0:T(128)} %starts_hbm.1, s32[4,1,128]{2,1,0:T(1,128)} %bitcast.1, f32[14,1024]{1,0:T(8,128)} %taper_hbm.1, bf16[1,32,17408]{2,1,0:T(8,128)(2,1)} %volts_hbm.1, bf16[1,8,32,2,512]{4,3,2,1,0:T(2,128)(2,1)} %weights_hbm.1, bf16[4,1024,256]{2,1,0:T(8,128)(2,1)} %constant.4.clone.table_hbm), custom_call_target="tpu_custom_call" | custom-call | tf_op jit(solution)/shard_map/pallas_call | solution.py:273
  12.9 3.2 %shard_map.74 = bf16[1,1,16,8,4,16,32]{6,5,4,3,2,1,0:T(8,128)(2,1)} custom-call(bf16[128,128]{1,0:T(8,128)(2,1)} %shard_map.73.beams_hbm, bf16[256,128]{1,0:T(8,128)(2,1)} %constant.5.clone.place_hbm), custom_call_target="tpu_custom_call" | custom-call | tf_op jit(solution)/shard_map/pallas_call | solution.py:306

commit v4 on v3

--- a/solution.py
+++ b/solution.py
@@ -96,20 +96,22 @@
     loads[1].wait()
     few = 4
 
-    def widen(step, carry):
+    chunks = length // LANES
+    share = beams * inputs // few // chunks
+
+    def widen(step):
         beam, at = lax.div(step, inputs // few), lax.rem(step, inputs // few)
         part = weights[beam, pl.ds(at * few, few)].astype(F32).reshape(2 * few, groups * group)
         for which in range(groups):
             wide[which, pl.ds(step * 2 * few, 2 * few), :] = part[:, which * group : (which + 1) * group]
-        return carry
-
-    lax.fori_loop(0, beams * inputs // few, widen, 0, unroll=4)
 
     loads[2].wait()
     loads[3].wait()
 
     def filter_chunk(chunk, carry):
         at = pl.multiple_of(chunk * LANES, LANES)
+        for step in range(share):
+            widen(chunk * share + step)
         sums = [None] * frames
         for segment in range(frames + taps - 1):
             lanes = pl.ds(pl.multiple_of(segment * length + at, LANES), LANES)
@@ -123,7 +125,7 @@
             filtered[frame * inputs : (frame + 1) * inputs, pl.ds(at, LANES)] = sums[frame].astype(BF16)
         return carry
 
-    lax.fori_loop(0, length // LANES, filter_chunk, 0)
+    lax.fori_loop(0, chunks, filter_chunk, 0)
 
     loads[4].wait()
     beam_row = lax.broadcasted_iota(jnp.int32, (beams, group), 0)
@@ -171,22 +173,25 @@
         base = which * group_targets
         outgoing[pl.ds(base, group_targets)] = ordered.astype(BF16).reshape(group_targets, rows, LANES)
 
-        def send(turn, carry):
-            part = lax.div(turn, stations)
+        def send(turn, carry, last=step == groups - 1, which=which, base=base):
+            part, turn = lax.div(turn, stations), lax.rem(turn, stations)
             to_st = lax.rem(st + turn, stations)
             target = base + part * stations + to_st
 
-            @pl.when(target != me)
-            def _():
+            def start():
                 pltpu.make_async_remote_copy(
                     src_ref=outgoing.at[target], dst_ref=arrived.at[me],
                     send_sem=send_sem, recv_sem=recv_sem,
                     device_id=(to_st, which * group_blocks + part), device_id_type=MESH,
                 ).start()
 
+            if last:
+                pl.when(target != me)(start)
+            else:
+                start()
             return carry
 
-        lax.fori_loop(0, group_targets, send, 0)
+        lax.fori_loop(0, group_targets, send, 0, unroll=math.gcd(8, group_targets))
 
     arrived[me] = outgoing[me]
     others = pl.ds(0, devices - 1)
@@ -244,7 +249,7 @@
         pltpu.make_async_copy(result.at[several], out_hbm.at[0, 0, several], sem).start()
         return carry
 
-    lax.fori_loop(0, per_owner // batch, channels, 0)
+    lax.fori_loop(0, per_owner // batch, channels, 0, unroll=True)
     pltpu.make_async_copy(result, out_hbm.at[0, 0], sem).wait()
 
 

time: 16.2 us -> 15.9 us (0.981)
  Pallas kernels: 16.1 us -> 15.7 us
    pallas_call x1, Pallas kernels: 3.16 us -> 2.89 us  [local(): pl.pallas_call(functools.partial(correlate_kernel, (beams, frames, per_ow...]
where the time goes in v4:
time: 15.9 us; the launch traced here: 15.7 us
  Pallas kernels  15.7 us (99%)
    pallas_call x1, Pallas kernels, local(): pl.pallas_call(functools.partial(beam_kernel, dims), out_shape=jax.ShapeD...  12.8 us
    pallas_call x1, Pallas kernels, local(): pl.pallas_call(functools.partial(correlate_kernel, (beams, frames, per_ow...  2.89 us

profile of v4, /device:TPU:0, one launch (start us, length us, event | category | flops | bytes accessed | tf_op | source)
XLA Modules:
  0.0 15.7 jit_solution(10031679140861550225)
XLA Ops:
  0.0 12.8 %shard_map.73.beams_hbm = bf16[128,128]{1,0:T(8,128)(2,1)} custom-call(s32[8]{0:T(128)} %starts_hbm.1, s32[4,1,128]{2,1,0:T(1,128)} %bitcast.1, f32[14,1024]{1,0:T(8,128)} %taper_hbm.1, bf16[1,32,17408]{2,1,0:T(8,128)(2,1)} %volts_hbm.1, bf16[1,8,32,2,512]{4,3,2,1,0:T(2,128)(2,1)} %weights_hbm.1, bf16[4,1024,256]{2,1,0:T(8,128)(2,1)} %constant.4.clone.table_hbm), custom_call_target="tpu_custom_call" | custom-call | tf_op jit(solution)/shard_map/pallas_call | solution.py:278
  12.8 2.9 %shard_map.74 = bf16[1,1,16,8,4,16,32]{6,5,4,3,2,1,0:T(8,128)(2,1)} custom-call(bf16[128,128]{1,0:T(8,128)(2,1)} %shard_map.73.beams_hbm, bf16[256,128]{1,0:T(8,128)(2,1)} %constant.5.clone.place_hbm), custom_call_target="tpu_custom_call" | custom-call | tf_op jit(solution)/shard_map/pallas_call | solution.py:311

commit v5 on v4

--- a/solution.py
+++ b/solution.py
@@ -142,7 +142,6 @@
 
     loads[5].wait()
     transform(0)
-    pl.semaphore_wait(barrier, devices - 1)
 
     for step in range(groups):
         which = turns[step]
@@ -172,6 +171,9 @@
         )
         base = which * group_targets
         outgoing[pl.ds(base, group_targets)] = ordered.astype(BF16).reshape(group_targets, rows, LANES)
+
+        if step == 0:
+            pl.semaphore_wait(barrier, devices - 1)
 
         def send(turn, carry, last=step == groups - 1, which=which, base=base):
             part, turn = lax.div(turn, stations), lax.rem(turn, stations)

time: 15.9 us -> 15.8 us (level)
  no operation moved by 1% of the time
where the time goes in v5:
time: 15.8 us; the launch traced here: 15.7 us
  Pallas kernels  15.7 us (99%)
    pallas_call x1, Pallas kernels, local(): pl.pallas_call(functools.partial(beam_kernel, dims), out_shape=jax.ShapeD...  12.8 us
    pallas_call x1, Pallas kernels, local(): pl.pallas_call(functools.partial(correlate_kernel, (beams, frames, per_ow...  2.89 us

profile of v5, /device:TPU:0, one launch (start us, length us, event | category | flops | bytes accessed | tf_op | source)
XLA Modules:
  0.0 15.7 jit_solution(8925343077300208507)
XLA Ops:
  0.0 12.8 %shard_map.73.beams_hbm = bf16[128,128]{1,0:T(8,128)(2,1)} custom-call(s32[8]{0:T(128)} %starts_hbm.1, s32[4,1,128]{2,1,0:T(1,128)} %bitcast.1, f32[14,1024]{1,0:T(8,128)} %taper_hbm.1, bf16[1,32,17408]{2,1,0:T(8,128)(2,1)} %volts_hbm.1, bf16[1,8,32,2,512]{4,3,2,1,0:T(2,128)(2,1)} %weights_hbm.1, bf16[4,1024,256]{2,1,0:T(8,128)(2,1)} %constant.4.clone.table_hbm), custom_call_target="tpu_custom_call" | custom-call | tf_op jit(solution)/shard_map/pallas_call | solution.py:280
  12.8 2.9 %shard_map.74 = bf16[1,1,16,8,4,16,32]{6,5,4,3,2,1,0:T(8,128)(2,1)} custom-call(bf16[128,128]{1,0:T(8,128)(2,1)} %shard_map.73.beams_hbm, bf16[256,128]{1,0:T(8,128)(2,1)} %constant.5.clone.place_hbm), custom_call_target="tpu_custom_call" | custom-call | tf_op jit(solution)/shard_map/pallas_call | solution.py:313

commit v6 on v5

--- a/solution.py
+++ b/solution.py
@@ -233,7 +233,7 @@
     right[:, :signals] = left[...]
     right[:, signals:] = turned.astype(BF16).reshape(per_owner, signals, LANES)
 
-    batch = math.gcd(4, per_owner)
+    batch = math.gcd(2, per_owner)
 
     def channels(step, carry):
         first = step * batch

time: 15.8 us -> 15.8 us (level)
  no operation moved by 1% of the time
where the time goes in v6:
time: 15.8 us; the launch traced here: 15.6 us
  Pallas kernels  15.6 us (99%)
    pallas_call x1, Pallas kernels, local(): pl.pallas_call(functools.partial(beam_kernel, dims), out_shape=jax.ShapeD...  12.8 us
    pallas_call x1, Pallas kernels, local(): pl.pallas_call(functools.partial(correlate_kernel, (beams, frames, per_ow...  2.82 us

profile of v6, /device:TPU:0, one launch (start us, length us, event | category | flops | bytes accessed | tf_op | source)
XLA Modules:
  0.0 15.6 jit_solution(178163051936666601)
XLA Ops:
  0.0 12.8 %shard_map.73.beams_hbm = bf16[128,128]{1,0:T(8,128)(2,1)} custom-call(s32[8]{0:T(128)} %starts_hbm.1, s32[4,1,128]{2,1,0:T(1,128)} %bitcast.1, f32[14,1024]{1,0:T(8,128)} %taper_hbm.1, bf16[1,32,17408]{2,1,0:T(8,128)(2,1)} %volts_hbm.1, bf16[1,8,32,2,512]{4,3,2,1,0:T(2,128)(2,1)} %weights_hbm.1, bf16[4,1024,256]{2,1,0:T(8,128)(2,1)} %constant.4.clone.table_hbm), custom_call_target="tpu_custom_call" | custom-call | tf_op jit(solution)/shard_map/pallas_call | solution.py:280
  12.8 2.8 %shard_map.74 = bf16[1,1,16,8,4,16,32]{6,5,4,3,2,1,0:T(8,128)(2,1)} custom-call(bf16[128,128]{1,0:T(8,128)(2,1)} %shard_map.73.beams_hbm, bf16[256,128]{1,0:T(8,128)(2,1)} %constant.5.clone.place_hbm), custom_call_target="tpu_custom_call" | custom-call | tf_op jit(solution)/shard_map/pallas_call | solution.py:313
